TPU v7x, 128 devices: a whole 4x4x4 slice. The times are simulated.
128 devices in a mesh: ctx: 16 (over y, x_hi, core), tp: 8 (over x_lo, z).
Axes of the slice: x: 4 (x_hi: 2, x_lo: 2; x = x_hi * 2 + x_lo), y: 4, z: 4, core: 2. Of those that a mesh axis runs over, the one named last changes fastest.
Arguments:
- normed_layer_input: bfloat16 [8192, 8192], P('ctx'), may hold values from -6 to 6
- queries: bfloat16 [8192, 8192], P('ctx', 'tp'), may hold values from -4.5 to 4.5
- keys: bfloat16 [8192, 1024], P('ctx', 'tp'), may hold values from -4.5 to 4.5
- values: bfloat16 [8192, 1024], P('ctx', 'tp'), may hold values from -6 to 6
- output_gradient: bfloat16 [8192, 8192], P('ctx', 'tp'), may hold values from -6 to 6
- positions: int32 [8192], P('ctx'), may hold values from 0 to 4095, as said below
- query_down_weight: bfloat16 [8, 8192], replicated, may hold values from -0.0625 to 0.0625
- query_up_weight: bfloat16 [8, 8192], P(None, 'tp'), may hold values from -0.0625 to 0.0625
- value_down_weight: bfloat16 [8, 8192], replicated, may hold values from -0.0625 to 0.0625
- value_up_weight: bfloat16 [8, 1024], P(None, 'tp'), may hold values from -0.1875 to 0.1875
Outputs:
- query_gradient_rows: bfloat16 [8192, 8192], P('ctx', 'tp')
- grad_keys: bfloat16 [8192, 1024], P('ctx', 'tp')
- value_gradient_rows: bfloat16 [8192, 1024], P('ctx', 'tp')
- grad_a_q: float32 [8, 8192], replicated
- grad_b_q: float32 [8, 8192], P(None, 'tp')
- grad_a_v: float32 [8, 8192], replicated
- grad_b_v: float32 [8, 1024], P(None, 'tp')
Inputs may be any that keep to these rules, and one draw needn't show every extreme that they name: `positions`: position ids count up by one from 0 within each packed sample; the first sample fills the first 4096 tokens and no later sample is longer.
All inputs are finite; a program needn't handle non-finite values.
Results may differ from a plain program's by a relative error of at most 0.02.
Values may be sent and summed in bfloat16 or wider, within the bound.
A program may use at most 128 MiB of HBM per device.

v0:
```python
import functools
import math

import jax
import jax.numpy as jnp
from jax import lax
from jax.experimental import pallas as pl
from jax.experimental.pallas import tpu as pltpu
from jax.sharding import PartitionSpec as P

QUERY_HEADS = 64
KEY_VALUE_HEADS = 8
FEATURES = 128
RANK = 8
SCALE_NUM = 1
SCALE_DEN = 8
ROPE_BASE = 10000.0
PLACES = 4
CHUNK = 256
HEADS = QUERY_HEADS // KEY_VALUE_HEADS
SCALE = FEATURES**-0.5
SCALE_LOG2 = SCALE * math.log2(math.e)

F32 = jnp.float32
BF16 = jnp.bfloat16
MESH = pl.DeviceIdType.MESH

SUMMED = {2: (0, 0), 3: (1, 1)}
SOURCES = {0: (1, 2), 1: (3,), 2: (3,), 3: ()}

DIRECT = {0: (1, 2), 1: (3,), 2: (3,), 3: ()}
HANDED = {2: (0, 3), 3: (1, 2)}


def nt(a, b):
    return lax.dot_general(a, b, (((1,), (1,)), ((), ())), preferred_element_type=F32)


def nn(a, b):
    return jnp.dot(a, b, preferred_element_type=F32)


def fold(a, op):
    return op(a.reshape(a.shape[0] // 8, 8, a.shape[1]), axis=0)


def kernel(
    n_ctx,
    n_tp,
    rows,
    x_hbm,
    q_hbm,
    k_hbm,
    v_hbm,
    do_hbm,
    pos_ref,
    dq_down_ref,
    up_q_ref,
    dv_down_ref,
    up_v_ref,
    dq_hbm,
    gk_hbm,
    gv_hbm,
    gb_hbm,
    full_hbm,
    xs,
    xr,
    kall,
    vall,
    ktr,
    vtr,
    qs,
    dos,
    dos_far,
    prob,
    work,
    peaks,
    deltas,
    dqs,
    dv_out,
    dv_in,
    dk_out,
    dk_in,
    dv_own,
    dk_own,
    ctab,
    stab,
    down,
    hid,
    pulls,
    gb_half,
    gb_in,
    gb_sums,
    gb_ref,
    ga_half,
    ga_in,
    ga_sums,
    full,
    gk_ref,
    gv_ref,
    load_sem,
    xsem,
    out_sem,
    own_sem,
    k_send,
    k_recv,
    v_send,
    v_recv,
    dv_send,
    dv_recv,
    dk_send,
    dk_recv,
    pull_send,
    pull_recv,
    sib_send,
    sib_recv,
    gbc_send,
    gbc_recv,
    gac_send,
    gac_recv,
    full_send,
    full_recv,
    hid_send,
    hid_recv,
):
    c = lax.axis_index("ctx")
    t = lax.axis_index("tp")
    halves = rows // CHUNK
    width = HEADS * FEATURES
    shifted = jnp.where(t >= n_tp // 2, PLACES // 2, 0)
    place = lax.rem(c + shifted, PLACES)

    def member(j):
        return lax.rem(c - place + j + n_ctx, n_ctx)

    barrier = pltpu.get_barrier_semaphore()
    core = lax.rem(c, 2)
    sibling = c + 1 - 2 * core
    chips = n_ctx // 2
    for peer in [sibling, member(PLACES - 1 - place)] + [lax.rem(c + 2 * d, n_ctx) for d in range(1, chips)]:
        pl.semaphore_signal(barrier, inc=1, device_id={"ctx": peer}, device_id_type=MESH)
    for d in range(1, n_tp):
        pl.semaphore_signal(barrier, inc=1, device_id={"tp": lax.rem(t + d, n_tp)}, device_id_type=MESH)

    own = pl.ds(pl.multiple_of(place * rows, rows), rows)
    own_k = pltpu.make_async_copy(k_hbm, kall.at[own], own_sem.at[0])
    own_v = pltpu.make_async_copy(v_hbm, vall.at[own], own_sem.at[1])
    own_k.start()
    loads = []
    for j in range(halves):
        for h in range(HEADS):
            for n, (src, dst) in enumerate(((q_hbm, qs), (do_hbm, dos))):
                loads.append(
                    pltpu.make_async_copy(
                        src.at[pl.ds(j * CHUNK, CHUNK), pl.ds(h * FEATURES, FEATURES)],
                        dst.at[j, pl.ds(h * CHUNK, CHUNK)],
                        load_sem.at[n, j * HEADS + h],
                    )
                )
    part = rows // n_tp
    load_rows = pltpu.make_async_copy(x_hbm.at[pl.ds(pl.multiple_of(t * part, part), part)], xr, xsem.at[0])
    load_share = pltpu.make_async_copy(x_hbm.at[:, pl.ds(pl.multiple_of(t * width, width), width)], xs, xsem.at[1])
    load_rows.start()
    for copy in loads:
        copy.start()
    own_v.start()
    load_share.start()

    pl.semaphore_wait(barrier, chips + n_tp)

    def block(b):
        return pl.ds(b * rows, rows)

    def send_block(src, dst, b, to, send, recv):
        return pltpu.make_async_remote_copy(
            src_ref=src,
            dst_ref=dst.at[block(b)],
            send_sem=send,
            recv_sem=recv.at[b],
            device_id={"ctx": member(to)},
            device_id_type=MESH,
        )

    for p in range(PLACES):

        @pl.when(place == p)
        def _(p=p):
            for i, to in enumerate(DIRECT[p]):
                send_block(k_hbm, kall, p, to, k_send.at[i], k_recv).start()

    lane = lax.broadcasted_iota(jnp.int32, (FEATURES, rows), 0)
    index = jnp.where(lane < FEATURES // 2, lane, lane - FEATURES // 2).astype(F32)
    inverse = jnp.exp(index * (-2.0 / FEATURES) * jnp.log(F32(ROPE_BASE)))
    angle = ((pos_ref[...] * SCALE_NUM).astype(F32) / SCALE_DEN) * inverse
    ctab[...] = jnp.cos(angle).T
    stab[...] = jnp.where(lane < FEATURES // 2, jnp.sin(angle), -jnp.sin(angle)).T

    ones = lax.broadcasted_iota(jnp.int32, (2 * RANK, PLACES * rows), 0) == 0
    vtr[FEATURES:, :] = jnp.where(ones, 1.0, 0.0).astype(BF16)
    down[...] = jnp.concatenate([dq_down_ref[...].astype(F32), dv_down_ref[...].astype(F32)], axis=0).astype(BF16)
    load_rows.wait()
    h = nt(xr[...], down[...])
    hid[t] = jnp.concatenate([h, jnp.zeros((part, FEATURES - 2 * RANK), F32)], axis=1).astype(BF16)

    def hid_copy(d):
        return pltpu.make_async_remote_copy(
            src_ref=hid.at[t],
            dst_ref=hid.at[t],
            send_sem=hid_send.at[d],
            recv_sem=hid_recv.at[t],
            device_id={"tp": lax.rem(t + d, n_tp)},
            device_id_type=MESH,
        )

    def hid_arrival(s):
        return pltpu.make_async_remote_copy(
            src_ref=hid.at[s],
            dst_ref=hid.at[s],
            send_sem=hid_send.at[0],
            recv_sem=hid_recv.at[s],
            device_id={"tp": s},
            device_id_type=MESH,
        )

    for d in range(1, n_tp):
        hid_copy(d).start()
    for p in range(PLACES):

        @pl.when(place == p)
        def _(p=p):
            for i, to in enumerate(DIRECT[p]):
                send_block(v_hbm, vall, p, to, v_send.at[i], v_recv).start()

    for copy in loads:
        copy.wait()
    own_k.wait()
    own_v.wait()

    causal = lax.broadcasted_iota(jnp.int32, (CHUNK, CHUNK), 0) <= lax.broadcasted_iota(jnp.int32, (CHUNK, CHUNK), 1)

    def unrotate(a, tokens):
        return a * ctab[tokens, :] + pltpu.roll(a, FEATURES // 2, 1) * stab[tokens, :]

    def attention(p):
        def tiles(j):
            return halves * p + j + 1

        def take(i):
            return pl.ds(i * CHUNK, CHUNK)

        def arrive(dst, send, recv, kind, done=None):
            src = k_hbm if kind == 0 else v_hbm
            if p in HANDED:
                b, to = HANDED[p]
                send_block(src, dst, b, to, send.at[2], recv).wait_recv()
                send_block(dst.at[block(b)], dst, b, to, send.at[2], recv).start()
            for b in range(p):
                if b != done and (p not in HANDED or b != HANDED[p][0]):
                    send_block(src, dst, b, b, send.at[0], recv).wait_recv()

        spans = [(0, 0, 2 * rows), (1, 2 * rows, None)] if p >= 2 else [(1, 0, None)]

        def span(g, j):
            _, a, b = next(s for s in spans if s[0] == g)
            return a, tiles(j) * CHUNK if b is None else b

        def softmax(g):
            @pl.loop(0, HEADS)
            def _(h):
                cols = pl.ds(pl.multiple_of(h * CHUNK, CHUNK), CHUNK)
                for j in range(halves):
                    query = qs[j, cols, :]
                    first, end = span(g, j)
                    last = end - CHUNK if g else end
                    starts = list(range(first, last, 2 * CHUNK)) + [last] * (g == 1)
                    peak = None
                    for a, b in zip(starts, starts[1:] + [end]):
                        s = nt(kall[a:b, :], query)
                        if g and a == last:
                            s = jnp.where(causal, s, -1e30)
                        work[j, a:b, :] = s
                        top = fold(s, jnp.max)
                        peak = top if peak is None else jnp.maximum(peak, top)
                    peak = jnp.max(peak, axis=0, keepdims=True) * SCALE_LOG2
                    peaks[g, j * HEADS + h] = peak
                    for a in range(first, end, CHUNK):
                        b = a + CHUNK
                        prob[j, a:b, cols] = jnp.exp2(work[j, a:b, :] * SCALE_LOG2 - peak).astype(BF16)

        near = {1: 0, 3: 2}
        if p in near:
            send_block(k_hbm, kall, near[p], near[p], k_send.at[0], k_recv).wait_recv()
        softmax(1)
        arrive(kall, k_send, k_recv, 0, near.get(p))
        for i in range(halves * (p + 1)):
            ktr[:, take(i)] = kall[take(i), :].astype(F32).T.astype(BF16)
        if p >= 2:
            softmax(0)

        scaled = (dos_far, dos)
        arrive(vall, v_send, v_recv, 1)
        for i in range(halves * (p + 1)):
            vtr[:FEATURES, take(i)] = vall[take(i), :].astype(F32).T.astype(BF16)

        @pl.loop(0, HEADS)
        def _(h):
            cols = pl.ds(pl.multiple_of(h * CHUNK, CHUNK), CHUNK)
            for j in range(halves):
                u = j * HEADS + h
                outs = {}
                for g, _, _ in spans:
                    a, b = span(g, j)
                    outs[g] = nn(vtr[:, a:b], prob[j, a:b, cols])
                if p >= 2:
                    peak = jnp.maximum(peaks[0, u], peaks[1, u])
                    factor = {g: jnp.exp2(peaks[g, u] - peak) for g in outs}
                    out = outs[0] * factor[0] + outs[1] * factor[1]
                    inv = 1.0 / out[FEATURES : FEATURES + 1]
                    factor = {g: factor[g] * inv for g in outs}
                else:
                    out = outs[1]
                    inv = 1.0 / out[FEATURES : FEATURES + 1]
                    factor = {1: inv}
                up = dos[j, cols, :].astype(F32).T
                delta = jnp.sum(up * out[:FEATURES], axis=0, keepdims=True) * inv
                for g in outs:
                    deltas[g, u] = delta * factor[g]
                    scaled[g][j, cols, :] = (up * factor[g]).T.astype(BF16)

        key_terms(p, range(p), True, (dos_far if p >= 2 else dos, dos), None, dv_out, dv_send, dv_in_recv, dv_own)

        @pl.loop(0, HEADS)
        def _(h):
            cols = pl.ds(pl.multiple_of(h * CHUNK, CHUNK), CHUNK)
            for j in range(halves):
                length = tiles(j) * CHUNK
                for g, _, _ in spans:
                    up = scaled[g][j, cols, :]
                    delta = deltas[g, j * HEADS + h]
                    first, end = span(g, j)
                    for a in range(first, end, 4 * CHUNK):
                        b = min(a + 4 * CHUNK, end)
                        m = nt(vall[a:b, :], up)
                        prob[j, a:b, cols] = (prob[j, a:b, cols].astype(F32) * (m - delta)).astype(BF16)
                grad = nn(ktr[:, :length], prob[j, :length, cols])
                out = unrotate(grad.T * SCALE, take(j))
                dqs[take(j), pl.ds(pl.multiple_of(h * FEATURES, FEATURES), FEATURES)] = out.astype(BF16)

        pltpu.make_async_copy(dqs, dq_hbm, out_sem.at[0]).start()

        total = dv_own[...]
        for src in range(p + 1, PLACES):
            term_copy(dv_out, dv_send, dv_in_recv, src, p).wait_recv()
            total = total + dv_in[src - 1].astype(F32)
        gv_ref[...] = total.astype(BF16)
        pltpu.make_async_copy(gv_ref, gv_hbm, out_sem.at[1]).start()

        pull = jnp.concatenate([nt(up_q_ref[...], dqs[...]), nt(up_v_ref[...], gv_ref[...])], axis=0)
        pulls[t] = pull.astype(BF16)
        for d in range(1, n_tp):
            pull_copy(d).start()

        key_terms(p, range(p), True, (qs, qs), SCALE, dk_out, dk_send, dk_in_recv, dk_own, SUMMED)

    def key_terms(p, blocks, home, right, scale, outs, send, into, kept, summed=()):
        def finish(a):
            return a if scale is None else a * scale

        for b in blocks:
            r = right[b // 2]
            a = nn(prob[0, block(b), :], r[0])
            for j in range(1, halves):
                a = a + nn(prob[j, block(b), :], r[j])
            outs[b] = finish(a).astype(BF16)
            if p not in summed or b != summed[p][0]:
                term_copy(outs, send, into, p, b, summed).start()
        if home:
            for i in range(halves):
                a = None
                for j in range(i, halves):
                    m = nn(prob[j, pl.ds((halves * p + i) * CHUNK, CHUNK), :], right[1][j])
                    a = m if a is None else a + m
                kept[pl.ds(i * CHUNK, CHUNK), :] = finish(a)

    dv_in_recv = (dv_in, dv_recv)
    dk_in_recv = (dk_in, dk_recv)

    def term_copy(outs, send, into, src, b, summed=()):
        dst, recv = into
        to, slot = b, src - 1
        if src in summed and b == summed[5 - src][0]:
            to, slot = 5 - src, summed[5 - src][1]
        return pltpu.make_async_remote_copy(
            src_ref=outs.at[b],
            dst_ref=dst.at[slot],
            send_sem=send.at[b],
            recv_sem=recv.at[slot],
            device_id={"ctx": member(to)},
            device_id_type=MESH,
        )

    def pull_copy(d):
        return pltpu.make_async_remote_copy(
            src_ref=pulls.at[t],
            dst_ref=pulls.at[t],
            send_sem=pull_send.at[d],
            recv_sem=pull_recv.at[t],
            device_id={"tp": lax.rem(t + d, n_tp)},
            device_id_type=MESH,
        )

    def pull_arrival(s):
        return pltpu.make_async_remote_copy(
            src_ref=pulls.at[s],
            dst_ref=pulls.at[s],
            send_sem=pull_send.at[0],
            recv_sem=pull_recv.at[s],
            device_id={"tp": s},
            device_id_type=MESH,
        )

    for p in range(PLACES):
        pl.when(place == p)(functools.partial(attention, p))

    for d in range(1, n_tp):
        hid_arrival(lax.rem(t + d, n_tp)).wait_recv()
    hidden = hid[...].astype(F32).reshape(rows, FEATURES).T[: 2 * RANK].astype(BF16)
    gb = nn(hidden, dqs[...])[:RANK]
    gbv = nn(hidden, gv_ref[...])[RANK:]
    half = width // 2
    for i in range(2):
        gb_half[i, :, :half] = gb[:, i * half : (i + 1) * half]
        gb_half[i, :, half:] = gbv

    def to_sibling(src, dst, n):
        return pltpu.make_async_remote_copy(
            src_ref=src,
            dst_ref=dst,
            send_sem=sib_send.at[n],
            recv_sem=sib_recv.at[n],
            device_id={"ctx": sibling},
            device_id_type=MESH,
        )

    gb_pair = to_sibling(gb_half.at[1 - core], gb_in, 0)
    gb_pair.start()

    for d in range(1, n_tp):
        pull_arrival(lax.rem(t + d, n_tp)).wait_recv()
    pull = pulls[0].astype(F32)
    for s in range(1, n_tp):
        pull = pull + pulls[s].astype(F32)
    high = pull.astype(BF16)
    low = (pull - high.astype(F32)).astype(BF16)
    load_share.wait()
    ga = nn(high, xs[...]) + nn(low, xs[...])
    for i in range(2):
        ga_half[i] = ga[:, i * half : (i + 1) * half]
    ga_pair = to_sibling(ga_half.at[1 - core], ga_in, 1)
    ga_pair.start()

    chip = c // 2

    def chip_copy(buf, send, recv, d):
        return pltpu.make_async_remote_copy(
            src_ref=buf.at[chip],
            dst_ref=buf.at[chip],
            send_sem=send.at[d],
            recv_sem=recv.at[chip],
            device_id={"ctx": lax.rem(c + 2 * d, n_ctx)},
            device_id_type=MESH,
        )

    def chip_arrival(buf, send, recv, d):
        other = lax.rem(chip + d, chips)
        return pltpu.make_async_remote_copy(
            src_ref=buf.at[other],
            dst_ref=buf.at[other],
            send_sem=send.at[0],
            recv_sem=recv.at[other],
            device_id={"ctx": lax.rem(c + 2 * d, n_ctx)},
            device_id_type=MESH,
        )

    gb_pair.wait_recv()
    gb_sums[chip] = gb_half[core] + gb_in[...]
    for d in range(1, chips):
        chip_copy(gb_sums, gbc_send, gbc_recv, d).start()
    ga_pair.wait_recv()
    ga_sums[chip] = (ga_half[core] + ga_in[...]).astype(BF16)
    for d in range(1, chips):
        chip_copy(ga_sums, gac_send, gac_recv, d).start()

    for d in range(1, chips):
        chip_arrival(ga_sums, gac_send, gac_recv, d).wait_recv()
    total = ga_sums[0].astype(F32)
    for i in range(1, chips):
        total = total + ga_sums[i].astype(F32)
    full[core, t] = total.astype(BF16)

    def full_copy(d):
        return pltpu.make_async_remote_copy(
            src_ref=full.at[core, t],
            dst_ref=full.at[core, t],
            send_sem=full_send.at[d],
            recv_sem=full_recv.at[t],
            device_id={"tp": lax.rem(t + d, n_tp)},
            device_id_type=MESH,
        )

    def full_arrival(s):
        return pltpu.make_async_remote_copy(
            src_ref=full.at[core, s],
            dst_ref=full.at[core, s],
            send_sem=full_send.at[0],
            recv_sem=full_recv.at[s],
            device_id={"tp": s},
            device_id_type=MESH,
        )

    for d in range(1, n_tp):
        full_copy(d).start()

    for p in range(PLACES):

        @pl.when(place == p)
        def _(p=p):
            if p in SUMMED:
                b, slot = SUMMED[p]
                term_copy(dk_out, dk_send, dk_in_recv, 5 - p, b, SUMMED).wait_recv()
                dk_out[b] = (dk_out[b].astype(F32) + dk_in[slot].astype(F32)).astype(BF16)
                term_copy(dk_out, dk_send, dk_in_recv, p, b, SUMMED).start()

    for d in range(1, chips):
        chip_arrival(gb_sums, gbc_send, gbc_recv, d).wait_recv()
    gb = gb_sums[0]
    for i in range(1, chips):
        gb = gb + gb_sums[i]
    gb_ref[core] = gb
    gb_other = to_sibling(gb_ref.at[core], gb_ref.at[core], 2)
    gb_other.start()

    gb_other.wait_recv()
    own_gb = pltpu.make_async_copy(gb_ref, gb_hbm, out_sem.at[4])
    own_gb.start()

    for d in range(1, n_tp):
        full_arrival(lax.rem(t + d, n_tp)).wait_recv()
    full_pair = to_sibling(full.at[core], full.at[core], 3)
    full_pair.start()
    own_share = pltpu.make_async_copy(full.at[core], full_hbm.at[core], out_sem.at[3])
    own_share.start()
    for p in range(PLACES):

        @pl.when(place == p)
        def _(p=p):
            total = dk_own[...]
            for src in SOURCES[p]:
                term_copy(dk_out, dk_send, dk_in_recv, src, p, SUMMED).wait_recv()
                total = total + dk_in[src - 1].astype(F32)
            gk_ref[...] = unrotate(total, pl.ds(0, rows)).astype(BF16)

    pltpu.make_async_copy(gk_ref, gk_hbm, out_sem.at[2]).start()
    full_pair.wait_recv()
    other_share = pltpu.make_async_copy(full.at[1 - core], full_hbm.at[1 - core], out_sem.at[5])
    other_share.start()

    for d in range(1, chips):
        chip_copy(gb_sums, gbc_send, gbc_recv, d).wait_send()
        chip_copy(ga_sums, gac_send, gac_recv, d).wait_send()
    for copy in (gb_pair, ga_pair, gb_other, full_pair):
        copy.wait_send()
    for d in range(1, n_tp):
        pull_copy(d).wait_send()
        hid_copy(d).wait_send()
        full_copy(d).wait_send()
    for p in range(PLACES):

        @pl.when(place == p)
        def _(p=p):
            for src, dst, send, recv in ((k_hbm, kall, k_send, k_recv), (v_hbm, vall, v_send, v_recv)):
                for i, to in enumerate(DIRECT[p]):
                    send_block(src, dst, p, to, send.at[i], recv).wait_send()
                if p in HANDED:
                    b, to = HANDED[p]
                    send_block(dst.at[block(b)], dst, b, to, send.at[2], recv).wait_send()
            for b in range(p):
                term_copy(dv_out, dv_send, dv_in_recv, p, b).wait_send()
                term_copy(dk_out, dk_send, dk_in_recv, p, b, SUMMED).wait_send()

    pltpu.make_async_copy(dqs, dq_hbm, out_sem.at[0]).wait()
    pltpu.make_async_copy(gv_ref, gv_hbm, out_sem.at[1]).wait()
    pltpu.make_async_copy(gk_ref, gk_hbm, out_sem.at[2]).wait()
    own_share.wait()
    other_share.wait()
    own_gb.wait()


def finish(dq_in, gk_in, gv_in, gb_in, full_in, dq, gk, gv, gaq, gbq, gav, gbv, dq_v, gk_v, gv_v, gb_v, full_v, ga_v, sem, out_sem):
    width = gbq.shape[1]
    rows = dq_in.shape[0]
    part = rows // finish_parts

    def piece(ref, i):
        return ref.at[pl.ds(i * part, part)]

    moves = [(piece(dq_in, i), piece(dq_v, i), piece(dq, i)) for i in range(finish_parts)]
    moves += [(gk_in, gk_v, gk), (gv_in, gv_v, gv)]
    loads = [pltpu.make_async_copy(a, b, sem.at[i]) for i, (a, b, _) in enumerate(moves)]
    stores = [pltpu.make_async_copy(b, c, out_sem.at[i]) for i, (_, b, c) in enumerate(moves)]
    n = len(moves)
    load_full = pltpu.make_async_copy(full_in, full_v, sem.at[n])
    load_gb = pltpu.make_async_copy(gb_in, gb_v, sem.at[n + 1])
    load_full.start()
    for load in loads:
        load.start()
    load_gb.start()
    for s in range(2):
        stores.append(pltpu.make_async_copy(ga_v.at[s], (gaq, gav)[s], out_sem.at[n + s]))
    load_full.wait()
    half = width // 2
    for s in range(full_in.shape[1]):
        for i in range(2):
            whole = full_v[i, s].astype(F32)
            a = s * width + i * half
            ga_v[0, :, a : a + half] = whole[:RANK]
            ga_v[1, :, a : a + half] = whole[RANK:]
    stores[n].start()
    stores[n + 1].start()
    for load, store in zip(loads, stores):
        load.wait()
        store.start()
    load_gb.wait()
    for i in range(2):
        stores.append(pltpu.make_async_copy(gb_v.at[i, :, pl.ds(0, half)], gbq.at[:, pl.ds(i * half, half)], out_sem.at[n + 2 + i]))
    stores.append(pltpu.make_async_copy(gb_v.at[0, :, pl.ds(half, FEATURES)], gbv, out_sem.at[n + 4]))
    for store in stores[n + 2 :]:
        store.start()
    for store in stores:
        store.wait()


finish_parts = 4


def shards(x, q, k, v, do, positions, down_q, up_q, down_v, up_v):
    n_ctx, n_tp = lax.axis_size("ctx"), lax.axis_size("tp")
    rows = q.shape[0]
    model = x.shape[1]
    keys = PLACES * rows
    halves = rows // CHUNK
    width = HEADS * FEATURES
    any_spec = pl.BlockSpec(memory_space=pl.ANY)
    vmem = pl.BlockSpec(memory_space=pltpu.VMEM)
    dma = pltpu.SemaphoreType.DMA
    terms = pltpu.VMEM((PLACES - 1, rows, FEATURES), BF16)
    whole = pltpu.VMEM((rows, FEATURES), F32)
    results = pl.pallas_call(
        functools.partial(kernel, n_ctx, n_tp, rows),
        out_shape=(
            jax.ShapeDtypeStruct((rows, width), BF16),
            jax.ShapeDtypeStruct((rows, FEATURES), BF16),
            jax.ShapeDtypeStruct((rows, FEATURES), BF16),
            jax.ShapeDtypeStruct((2, RANK, width // 2 + FEATURES), F32),
            jax.ShapeDtypeStruct((2, n_tp, 2 * RANK, width // 2), BF16),
        ),
        in_specs=[any_spec] * 5 + [vmem] * 5,
        out_specs=(any_spec,) * 5,
        scratch_shapes=[
            pltpu.VMEM((rows, width), BF16),
            pltpu.VMEM((rows // n_tp, model), BF16),
            pltpu.VMEM((keys, FEATURES), BF16),
            pltpu.VMEM((keys, FEATURES), BF16),
            pltpu.VMEM((FEATURES, keys), BF16),
            pltpu.VMEM((FEATURES + 2 * RANK, keys), BF16),
            pltpu.VMEM((halves, HEADS * CHUNK, FEATURES), BF16),
            pltpu.VMEM((halves, HEADS * CHUNK, FEATURES), BF16),
            pltpu.VMEM((halves, HEADS * CHUNK, FEATURES), BF16),
            pltpu.VMEM((halves, keys, HEADS * CHUNK), BF16),
            pltpu.VMEM((halves, keys, CHUNK), F32),
            pltpu.VMEM((2, halves * HEADS, 1, CHUNK), F32),
            pltpu.VMEM((2, halves * HEADS, 1, CHUNK), F32),
            pltpu.VMEM((rows, width), BF16),
            terms,
            terms,
            terms,
            terms,
            whole,
            whole,
            whole,
            whole,
            pltpu.VMEM((2 * RANK, model), BF16),
            pltpu.VMEM((n_tp, rows // n_tp, FEATURES), BF16),
            pltpu.VMEM((n_tp, 2 * RANK, rows), BF16),
            pltpu.VMEM((2, RANK, width // 2 + FEATURES), F32),
            pltpu.VMEM((RANK, width // 2 + FEATURES), F32),
            pltpu.VMEM((n_ctx // 2, RANK, width // 2 + FEATURES), F32),
            pltpu.VMEM((2, RANK, width // 2 + FEATURES), F32),
            pltpu.VMEM((2, 2 * RANK, width // 2), F32),
            pltpu.VMEM((2 * RANK, width // 2), F32),
            pltpu.VMEM((n_ctx // 2, 2 * RANK, width // 2), BF16),
            pltpu.VMEM((2, n_tp, 2 * RANK, width // 2), BF16),
            pltpu.VMEM((rows, FEATURES), BF16),
            pltpu.VMEM((rows, FEATURES), BF16),
            dma((2, halves * HEADS)),
            dma((2,)),
            dma((6,)),
            dma((2,)),
            dma((3,)),
            dma((PLACES,)),
            dma((3,)),
            dma((PLACES,)),
            dma((PLACES - 1,)),
            dma((PLACES - 1,)),
            dma((PLACES - 1,)),
            dma((PLACES - 1,)),
            dma((n_tp,)),
            dma((n_tp,)),
            dma((4,)),
            dma((4,)),
            dma((n_ctx // 2,)),
            dma((n_ctx // 2,)),
            dma((n_ctx // 2,)),
            dma((n_ctx // 2,)),
            dma((n_tp,)),
            dma((n_tp,)),
            dma((n_tp,)),
            dma((n_tp,)),
        ],
        compiler_params=pltpu.CompilerParams(
            collective_id=0, has_side_effects=True, vmem_limit_bytes=56 * 1024 * 1024
        ),
        cost_estimate=pl.CostEstimate(flops=12 * 10**9, bytes_accessed=16 * 10**6, transcendentals=8 * 10**6),
    )(x, q, k, v, do, positions.reshape(1, rows), down_q, up_q, down_v, up_v)
    return pl.pallas_call(
        finish,
        out_shape=(
            jax.ShapeDtypeStruct((rows, width), BF16),
            jax.ShapeDtypeStruct((rows, FEATURES), BF16),
            jax.ShapeDtypeStruct((rows, FEATURES), BF16),
            jax.ShapeDtypeStruct((RANK, model), F32),
            jax.ShapeDtypeStruct((RANK, width), F32),
            jax.ShapeDtypeStruct((RANK, model), F32),
            jax.ShapeDtypeStruct((RANK, FEATURES), F32),
        ),
        in_specs=[any_spec] * 5,
        out_specs=(any_spec,) * 7,
        scratch_shapes=[
            pltpu.VMEM((rows, width), BF16),
            pltpu.VMEM((rows, FEATURES), BF16),
            pltpu.VMEM((rows, FEATURES), BF16),
            pltpu.VMEM((2, RANK, width // 2 + FEATURES), F32),
            pltpu.VMEM((2, n_tp, 2 * RANK, width // 2), BF16),
            pltpu.VMEM((2, RANK, model), F32),
            dma((finish_parts + 4,)),
            dma((finish_parts + 7,)),
        ],
        compiler_params=pltpu.CompilerParams(vmem_limit_bytes=56 * 1024 * 1024),
    )(*results)


def solution(mesh):
    in_specs = (
        P("ctx", None),
        P("ctx", "tp"),
        P("ctx", "tp"),
        P("ctx", "tp"),
        P("ctx", "tp"),
        P("ctx"),
        P(),
        P(None, "tp"),
        P(),
        P(None, "tp"),
    )
    out_specs = (
        P("ctx", "tp"),
        P("ctx", "tp"),
        P("ctx", "tp"),
        P(),
        P(None, "tp"),
        P(),
        P(None, "tp"),
    )
    return jax.shard_map(shards, mesh=mesh, in_specs=in_specs, out_specs=out_specs, check_vma=False)
```

profile of v0, /device:TPU:1, one launch (start us, length us, event | category | flops | bytes accessed | tf_op | source)
XLA Modules:
  0.0 74.5 jit_solution(15380490686615980967)
XLA Ops:
  0.6 71.2 %shard_map.153 = (bf16[512,1024]{1,0:T(8,128)(2,1)}, bf16[512,128]{1,0:T(8,128)(2,1)}, bf16[512,128]{1,0:T(8,128)(2,1)}, f32[2,8,640]{2,1,0:T(8,128)}, bf16[2,8,16,512]{3,2,1,0:T(8,128)(2,1)}) custom-call(bf16[512,8192]{1,0:T(8,128)(2,1)} %x_hbm.1, bf16[512,1024]{1,0:T(8,128)(2,1)} %q_hbm.1, bf16[512,128]{1,0:T(8,128)(2,1)} %k_hbm.1, ...), custom_call_target="tpu_custom_call" | custom-call | flops 12000000000 | bytes 16000000 | tf_op jit(solution)/shard_map/pallas_call | solution.py:658
  71.9 2.4 %shard_map.154 = (bf16[512,1024]{1,0:T(8,128)(2,1)}, bf16[512,128]{1,0:T(8,128)(2,1)}, bf16[512,128]{1,0:T(8,128)(2,1)}, f32[8,8192]{1,0:T(8,128)}, f32[8,1024]{...) custom-call(bf16[512,1024]{1,0:T(8,128)(2,1)} %get-tuple-element.12.dq_in, bf16[512,128]{1,0:T(8,128)(2,1)} %get-tuple-element.13.gk_in, ...), custom_call_target="tpu_custom_call" | custom-call | tf_op jit(solution)/shard_map/pallas_call | solution.py:735
where the time goes:
time: 74.6 us; the launch traced here: 74.5 us
  Pallas kernels  73.6 us (99%)
  between operations  0.86 us (1%)
    pallas_call x1, Pallas kernels, shards(): pl.pallas_call(functools.partial(kernel, n_ctx, n_tp, rows), out_shape=(j...  71.2 us
    pallas_call x1, Pallas kernels, shards(): pl.pallas_call(finish, out_shape=(jax.ShapeDtypeStruct((rows, width), BF1...  2.38 us

commit v1 on v0

--- a/solution.py
+++ b/solution.py
@@ -71,7 +71,6 @@
     vtr,
     qs,
     dos,
-    dos_far,
     prob,
     work,
     peaks,
@@ -149,7 +148,7 @@
     loads = []
     for j in range(halves):
         for h in range(HEADS):
-            for n, (src, dst) in enumerate(((q_hbm, qs), (do_hbm, dos))):
+            for n, (src, dst) in enumerate(((q_hbm, qs), (do_hbm, dos.at[1]))):
                 loads.append(
                     pltpu.make_async_copy(
                         src.at[pl.ds(j * CHUNK, CHUNK), pl.ds(h * FEATURES, FEATURES)],
@@ -188,12 +187,12 @@
             for i, to in enumerate(DIRECT[p]):
                 send_block(k_hbm, kall, p, to, k_send.at[i], k_recv).start()
 
-    lane = lax.broadcasted_iota(jnp.int32, (FEATURES, rows), 0)
-    index = jnp.where(lane < FEATURES // 2, lane, lane - FEATURES // 2).astype(F32)
+    index = lax.broadcasted_iota(jnp.int32, (FEATURES // 2, rows), 0).astype(F32)
     inverse = jnp.exp(index * (-2.0 / FEATURES) * jnp.log(F32(ROPE_BASE)))
     angle = ((pos_ref[...] * SCALE_NUM).astype(F32) / SCALE_DEN) * inverse
-    ctab[...] = jnp.cos(angle).T
-    stab[...] = jnp.where(lane < FEATURES // 2, jnp.sin(angle), -jnp.sin(angle)).T
+    cosine, sine = jnp.cos(angle), jnp.sin(angle)
+    ctab[...] = jnp.concatenate([cosine, cosine], axis=0).T
+    stab[...] = jnp.concatenate([sine, -sine], axis=0).T
 
     ones = lax.broadcasted_iota(jnp.int32, (2 * RANK, PLACES * rows), 0) == 0
     vtr[FEATURES:, :] = jnp.where(ones, 1.0, 0.0).astype(BF16)
@@ -240,6 +239,15 @@
 
     def unrotate(a, tokens):
         return a * ctab[tokens, :] + pltpu.roll(a, FEATURES // 2, 1) * stab[tokens, :]
+
+    def spans_of(p):
+        spans = [(0, 0, 2 * rows), (1, 2 * rows, None)] if p >= 2 else [(1, 0, None)]
+
+        def span(g, j):
+            _, a, b = next(s for s in spans if s[0] == g)
+            return a, (halves * p + j + 1) * CHUNK if b is None else b
+
+        return spans, span
 
     def attention(p):
         def tiles(j):
@@ -258,11 +266,7 @@
                 if b != done and (p not in HANDED or b != HANDED[p][0]):
                     send_block(src, dst, b, b, send.at[0], recv).wait_recv()
 
-        spans = [(0, 0, 2 * rows), (1, 2 * rows, None)] if p >= 2 else [(1, 0, None)]
-
-        def span(g, j):
-            _, a, b = next(s for s in spans if s[0] == g)
-            return a, tiles(j) * CHUNK if b is None else b
+        spans, span = spans_of(p)
 
         def softmax(g):
             @pl.loop(0, HEADS)
@@ -293,14 +297,13 @@
         softmax(1)
         arrive(kall, k_send, k_recv, 0, near.get(p))
         for i in range(halves * (p + 1)):
-            ktr[:, take(i)] = kall[take(i), :].astype(F32).T.astype(BF16)
+            ktr[:, take(i)] = kall[take(i), :].T
         if p >= 2:
             softmax(0)
 
-        scaled = (dos_far, dos)
         arrive(vall, v_send, v_recv, 1)
         for i in range(halves * (p + 1)):
-            vtr[:FEATURES, take(i)] = vall[take(i), :].astype(F32).T.astype(BF16)
+            vtr[:FEATURES, take(i)] = vall[take(i), :].T
 
         @pl.loop(0, HEADS)
         def _(h):
@@ -321,13 +324,20 @@
                     out = outs[1]
                     inv = 1.0 / out[FEATURES : FEATURES + 1]
                     factor = {1: inv}
-                up = dos[j, cols, :].astype(F32).T
+                up = dos[1, j, cols, :].T.astype(F32)
                 delta = jnp.sum(up * out[:FEATURES], axis=0, keepdims=True) * inv
                 for g in outs:
                     deltas[g, u] = delta * factor[g]
-                    scaled[g][j, cols, :] = (up * factor[g]).T.astype(BF16)
-
-        key_terms(p, range(p), True, (dos_far if p >= 2 else dos, dos), None, dv_out, dv_send, dv_in_recv, dv_own)
+                    dos[g, j, cols, :] = (up * factor[g]).astype(BF16).T
+
+    def query_terms(p):
+        def tiles(j):
+            return halves * p + j + 1
+
+        def take(i):
+            return pl.ds(i * CHUNK, CHUNK)
+
+        spans, span = spans_of(p)
 
         @pl.loop(0, HEADS)
         def _(h):
@@ -335,7 +345,7 @@
             for j in range(halves):
                 length = tiles(j) * CHUNK
                 for g, _, _ in spans:
-                    up = scaled[g][j, cols, :]
+                    up = dos[g, j, cols, :]
                     delta = deltas[g, j * HEADS + h]
                     first, end = span(g, j)
                     for a in range(first, end, 4 * CHUNK):
@@ -346,41 +356,47 @@
                 out = unrotate(grad.T * SCALE, take(j))
                 dqs[take(j), pl.ds(pl.multiple_of(h * FEATURES, FEATURES), FEATURES)] = out.astype(BF16)
 
-        pltpu.make_async_copy(dqs, dq_hbm, out_sem.at[0]).start()
-
-        total = dv_own[...]
-        for src in range(p + 1, PLACES):
-            term_copy(dv_out, dv_send, dv_in_recv, src, p).wait_recv()
-            total = total + dv_in[src - 1].astype(F32)
-        gv_ref[...] = total.astype(BF16)
-        pltpu.make_async_copy(gv_ref, gv_hbm, out_sem.at[1]).start()
-
-        pull = jnp.concatenate([nt(up_q_ref[...], dqs[...]), nt(up_v_ref[...], gv_ref[...])], axis=0)
-        pulls[t] = pull.astype(BF16)
-        for d in range(1, n_tp):
-            pull_copy(d).start()
-
-        key_terms(p, range(p), True, (qs, qs), SCALE, dk_out, dk_send, dk_in_recv, dk_own, SUMMED)
-
-    def key_terms(p, blocks, home, right, scale, outs, send, into, kept, summed=()):
+    def key_terms(right, scale, outs, send, into, kept, summed):
         def finish(a):
             return a if scale is None else a * scale
 
-        for b in blocks:
-            r = right[b // 2]
-            a = nn(prob[0, block(b), :], r[0])
+        def product(first, length, j, g):
+            return nn(prob[j, pl.ds(pl.multiple_of(first, CHUNK), length), :], right(j, g))
+
+        def other(b, carry):
+            g = jnp.where((place >= 2) & (b < 2), 0, 1)
+            a = product(b * rows, rows, 0, g)
             for j in range(1, halves):
-                a = a + nn(prob[j, block(b), :], r[j])
+                a = a + product(b * rows, rows, j, g)
             outs[b] = finish(a).astype(BF16)
-            if p not in summed or b != summed[p][0]:
-                term_copy(outs, send, into, p, b, summed).start()
-        if home:
-            for i in range(halves):
-                a = None
-                for j in range(i, halves):
-                    m = nn(prob[j, pl.ds((halves * p + i) * CHUNK, CHUNK), :], right[1][j])
-                    a = m if a is None else a + m
-                kept[pl.ds(i * CHUNK, CHUNK), :] = finish(a)
+            dst, recv = into
+            held = place < 0
+            to, slot = b, place - 1
+            if summed:
+                cross = (place >= 2) & (b < 2)
+                held = cross & (b == place - 2)
+                to, slot = jnp.where(cross, 5 - place, b), jnp.where(cross, b, place - 1)
+
+            @pl.when(jnp.logical_not(held))
+            def _():
+                pltpu.make_async_remote_copy(
+                    src_ref=outs.at[b],
+                    dst_ref=dst.at[slot],
+                    send_sem=send.at[b],
+                    recv_sem=recv.at[slot],
+                    device_id={"ctx": member(to)},
+                    device_id_type=MESH,
+                ).start()
+
+            return carry
+
+        lax.fori_loop(0, place, other, 0)
+        for i in range(halves):
+            a = None
+            for j in range(i, halves):
+                m = product(place * rows + i * CHUNK, CHUNK, j, 1)
+                a = m if a is None else a + m
+            kept[pl.ds(i * CHUNK, CHUNK), :] = finish(a)
 
     dv_in_recv = (dv_in, dv_recv)
     dk_in_recv = (dk_in, dk_recv)
@@ -421,6 +437,29 @@
 
     for p in range(PLACES):
         pl.when(place == p)(functools.partial(attention, p))
+    key_terms(lambda j, g: dos[g, j], None, dv_out, dv_send, dv_in_recv, dv_own, False)
+    for p in range(PLACES):
+        pl.when(place == p)(functools.partial(query_terms, p))
+    pltpu.make_async_copy(dqs, dq_hbm, out_sem.at[0]).start()
+
+    for p in range(PLACES):
+
+        @pl.when(place == p)
+        def _(p=p):
+            total = dv_own[...]
+            for src in range(p + 1, PLACES):
+                term_copy(dv_out, dv_send, dv_in_recv, src, p).wait_recv()
+                total = total + dv_in[src - 1].astype(F32)
+            gv_ref[...] = total.astype(BF16)
+
+    pltpu.make_async_copy(gv_ref, gv_hbm, out_sem.at[1]).start()
+
+    pull = jnp.concatenate([nt(up_q_ref[...], dqs[...]), nt(up_v_ref[...], gv_ref[...])], axis=0)
+    pulls[t] = pull.astype(BF16)
+    for d in range(1, n_tp):
+        pull_copy(d).start()
+
+    key_terms(lambda j, g: qs[j], SCALE, dk_out, dk_send, dk_in_recv, dk_own, True)
 
     for d in range(1, n_tp):
         hid_arrival(lax.rem(t + d, n_tp)).wait_recv()
@@ -674,8 +713,7 @@
             pltpu.VMEM((FEATURES, keys), BF16),
             pltpu.VMEM((FEATURES + 2 * RANK, keys), BF16),
             pltpu.VMEM((halves, HEADS * CHUNK, FEATURES), BF16),
-            pltpu.VMEM((halves, HEADS * CHUNK, FEATURES), BF16),
-            pltpu.VMEM((halves, HEADS * CHUNK, FEATURES), BF16),
+            pltpu.VMEM((2, halves, HEADS * CHUNK, FEATURES), BF16),
             pltpu.VMEM((halves, keys, HEADS * CHUNK), BF16),
             pltpu.VMEM((halves, keys, CHUNK), F32),
             pltpu.VMEM((2, halves * HEADS, 1, CHUNK), F32),

time: 74.6 us -> 68.7 us (0.921)
  Pallas kernels: 73.6 us -> 67.7 us
    pallas_call x1, Pallas kernels: 71.2 us -> 65.4 us  [shards(): pl.pallas_call(functools.partial(kernel, n_ctx, n_tp, rows), out_shape=(j...]
where the time goes in v1:
time: 68.7 us; the launch traced here: 68.6 us
  Pallas kernels  67.7 us (99%)
  between operations  0.8 us (1%)
    pallas_call x1, Pallas kernels, shards(): pl.pallas_call(functools.partial(kernel, n_ctx, n_tp, rows), out_shape=(j...  65.4 us
    pallas_call x1, Pallas kernels, shards(): pl.pallas_call(finish, out_shape=(jax.ShapeDtypeStruct((rows, width), BF1...  2.38 us

profile of v1, /device:TPU:1, one launch (start us, length us, event | category | flops | bytes accessed | tf_op | source)
XLA Modules:
  0.0 68.6 jit_solution(7251851356018819265)
XLA Ops:
  0.6 65.4 %shard_map.153 = (bf16[512,1024]{1,0:T(8,128)(2,1)}, bf16[512,128]{1,0:T(8,128)(2,1)}, bf16[512,128]{1,0:T(8,128)(2,1)}, f32[2,8,640]{2,1,0:T(8,128)}, bf16[2,8,16,512]{3,2,1,0:T(8,128)(2,1)}) custom-call(bf16[512,8192]{1,0:T(8,128)(2,1)} %x_hbm.1, bf16[512,1024]{1,0:T(8,128)(2,1)} %q_hbm.1, bf16[512,128]{1,0:T(8,128)(2,1)} %k_hbm.1, ...), custom_call_target="tpu_custom_call" | custom-call | flops 12000000000 | bytes 16000000 | tf_op jit(solution)/shard_map/pallas_call | solution.py:697
  66.0 2.4 %shard_map.154 = (bf16[512,1024]{1,0:T(8,128)(2,1)}, bf16[512,128]{1,0:T(8,128)(2,1)}, bf16[512,128]{1,0:T(8,128)(2,1)}, f32[8,8192]{1,0:T(8,128)}, f32[8,1024]{...) custom-call(bf16[512,1024]{1,0:T(8,128)(2,1)} %get-tuple-element.12.dq_in, bf16[512,128]{1,0:T(8,128)(2,1)} %get-tuple-element.13.gk_in, ...), custom_call_target="tpu_custom_call" | custom-call | tf_op jit(solution)/shard_map/pallas_call | solution.py:773

commit v2 on v1

--- a/solution.py
+++ b/solution.py
@@ -269,27 +269,28 @@
         spans, span = spans_of(p)
 
         def softmax(g):
-            @pl.loop(0, HEADS)
-            def _(h):
-                cols = pl.ds(pl.multiple_of(h * CHUNK, CHUNK), CHUNK)
-                for j in range(halves):
-                    query = qs[j, cols, :]
-                    first, end = span(g, j)
-                    last = end - CHUNK if g else end
-                    starts = list(range(first, last, 2 * CHUNK)) + [last] * (g == 1)
-                    peak = None
-                    for a, b in zip(starts, starts[1:] + [end]):
-                        s = nt(kall[a:b, :], query)
-                        if g and a == last:
-                            s = jnp.where(causal, s, -1e30)
-                        work[j, a:b, :] = s
-                        top = fold(s, jnp.max)
-                        peak = top if peak is None else jnp.maximum(peak, top)
-                    peak = jnp.max(peak, axis=0, keepdims=True) * SCALE_LOG2
-                    peaks[g, j * HEADS + h] = peak
-                    for a in range(first, end, CHUNK):
-                        b = a + CHUNK
-                        prob[j, a:b, cols] = jnp.exp2(work[j, a:b, :] * SCALE_LOG2 - peak).astype(BF16)
+            @pl.loop(0, HEADS // 2)
+            def _(h0):
+                for h in [h0 * 2 + i for i in range(2)]:
+                    cols = pl.ds(pl.multiple_of(h * CHUNK, CHUNK), CHUNK)
+                    for j in range(halves):
+                        query = qs[j, cols, :]
+                        first, end = span(g, j)
+                        last = end - CHUNK if g else end
+                        starts = list(range(first, last, 2 * CHUNK)) + [last] * (g == 1)
+                        peak = None
+                        for a, b in zip(starts, starts[1:] + [end]):
+                            s = nt(kall[a:b, :], query)
+                            if g and a == last:
+                                s = jnp.where(causal, s, -1e30)
+                            work[j, a:b, :] = s
+                            top = fold(s, jnp.max)
+                            peak = top if peak is None else jnp.maximum(peak, top)
+                        peak = jnp.max(peak, axis=0, keepdims=True) * SCALE_LOG2
+                        peaks[g, j * HEADS + h] = peak
+                        for a in range(first, end, CHUNK):
+                            b = a + CHUNK
+                            prob[j, a:b, cols] = jnp.exp2(work[j, a:b, :] * SCALE_LOG2 - peak).astype(BF16)
 
         near = {1: 0, 3: 2}
         if p in near:
@@ -305,30 +306,31 @@
         for i in range(halves * (p + 1)):
             vtr[:FEATURES, take(i)] = vall[take(i), :].T
 
-        @pl.loop(0, HEADS)
-        def _(h):
-            cols = pl.ds(pl.multiple_of(h * CHUNK, CHUNK), CHUNK)
-            for j in range(halves):
-                u = j * HEADS + h
-                outs = {}
-                for g, _, _ in spans:
-                    a, b = span(g, j)
-                    outs[g] = nn(vtr[:, a:b], prob[j, a:b, cols])
-                if p >= 2:
-                    peak = jnp.maximum(peaks[0, u], peaks[1, u])
-                    factor = {g: jnp.exp2(peaks[g, u] - peak) for g in outs}
-                    out = outs[0] * factor[0] + outs[1] * factor[1]
-                    inv = 1.0 / out[FEATURES : FEATURES + 1]
-                    factor = {g: factor[g] * inv for g in outs}
-                else:
-                    out = outs[1]
-                    inv = 1.0 / out[FEATURES : FEATURES + 1]
-                    factor = {1: inv}
-                up = dos[1, j, cols, :].T.astype(F32)
-                delta = jnp.sum(up * out[:FEATURES], axis=0, keepdims=True) * inv
-                for g in outs:
-                    deltas[g, u] = delta * factor[g]
-                    dos[g, j, cols, :] = (up * factor[g]).astype(BF16).T
+        @pl.loop(0, HEADS // 2)
+        def _(h0):
+            for h in [h0 * 2 + i for i in range(2)]:
+                cols = pl.ds(pl.multiple_of(h * CHUNK, CHUNK), CHUNK)
+                for j in range(halves):
+                    u = j * HEADS + h
+                    outs = {}
+                    for g, _, _ in spans:
+                        a, b = span(g, j)
+                        outs[g] = nn(vtr[:, a:b], prob[j, a:b, cols])
+                    if p >= 2:
+                        peak = jnp.maximum(peaks[0, u], peaks[1, u])
+                        factor = {g: jnp.exp2(peaks[g, u] - peak) for g in outs}
+                        out = outs[0] * factor[0] + outs[1] * factor[1]
+                        inv = 1.0 / out[FEATURES : FEATURES + 1]
+                        factor = {g: factor[g] * inv for g in outs}
+                    else:
+                        out = outs[1]
+                        inv = 1.0 / out[FEATURES : FEATURES + 1]
+                        factor = {1: inv}
+                    up = dos[1, j, cols, :].T.astype(F32)
+                    delta = jnp.sum(up * out[:FEATURES], axis=0, keepdims=True) * inv
+                    for g in outs:
+                        deltas[g, u] = delta * factor[g]
+                        dos[g, j, cols, :] = (up * factor[g]).astype(BF16).T
 
     def query_terms(p):
         def tiles(j):
@@ -339,22 +341,23 @@
 
         spans, span = spans_of(p)
 
-        @pl.loop(0, HEADS)
-        def _(h):
-            cols = pl.ds(pl.multiple_of(h * CHUNK, CHUNK), CHUNK)
-            for j in range(halves):
-                length = tiles(j) * CHUNK
-                for g, _, _ in spans:
-                    up = dos[g, j, cols, :]
-                    delta = deltas[g, j * HEADS + h]
-                    first, end = span(g, j)
-                    for a in range(first, end, 4 * CHUNK):
-                        b = min(a + 4 * CHUNK, end)
-                        m = nt(vall[a:b, :], up)
-                        prob[j, a:b, cols] = (prob[j, a:b, cols].astype(F32) * (m - delta)).astype(BF16)
-                grad = nn(ktr[:, :length], prob[j, :length, cols])
-                out = unrotate(grad.T * SCALE, take(j))
-                dqs[take(j), pl.ds(pl.multiple_of(h * FEATURES, FEATURES), FEATURES)] = out.astype(BF16)
+        @pl.loop(0, HEADS // 2)
+        def _(h0):
+            for h in [h0 * 2 + i for i in range(2)]:
+                cols = pl.ds(pl.multiple_of(h * CHUNK, CHUNK), CHUNK)
+                for j in range(halves):
+                    length = tiles(j) * CHUNK
+                    for g, _, _ in spans:
+                        up = dos[g, j, cols, :]
+                        delta = deltas[g, j * HEADS + h]
+                        first, end = span(g, j)
+                        for a in range(first, end, 4 * CHUNK):
+                            b = min(a + 4 * CHUNK, end)
+                            m = nt(vall[a:b, :], up)
+                            prob[j, a:b, cols] = (prob[j, a:b, cols].astype(F32) * (m - delta)).astype(BF16)
+                    grad = nn(ktr[:, :length], prob[j, :length, cols])
+                    out = unrotate(grad.T * SCALE, take(j))
+                    dqs[take(j), pl.ds(pl.multiple_of(h * FEATURES, FEATURES), FEATURES)] = out.astype(BF16)
 
     def key_terms(right, scale, outs, send, into, kept, summed):
         def finish(a):
@@ -459,8 +462,6 @@
     for d in range(1, n_tp):
         pull_copy(d).start()
 
-    key_terms(lambda j, g: qs[j], SCALE, dk_out, dk_send, dk_in_recv, dk_own, True)
-
     for d in range(1, n_tp):
         hid_arrival(lax.rem(t + d, n_tp)).wait_recv()
     hidden = hid[...].astype(F32).reshape(rows, FEATURES).T[: 2 * RANK].astype(BF16)
@@ -483,6 +484,8 @@
 
     gb_pair = to_sibling(gb_half.at[1 - core], gb_in, 0)
     gb_pair.start()
+
+    key_terms(lambda j, g: qs[j], SCALE, dk_out, dk_send, dk_in_recv, dk_own, True)
 
     for d in range(1, n_tp):
         pull_arrival(lax.rem(t + d, n_tp)).wait_recv()

time: 68.7 us -> 62.7 us (0.913)
  Pallas kernels: 67.7 us -> 61.8 us
    pallas_call x1, Pallas kernels: 65.4 us -> 59.4 us  [shards(): pl.pallas_call(functools.partial(kernel, n_ctx, n_tp, rows), out_shape=(j...]
where the time goes in v2:
time: 62.7 us; the launch traced here: 62.6 us
  Pallas kernels  61.8 us (99%)
  between operations  0.8 us (1%)
    pallas_call x1, Pallas kernels, shards(): pl.pallas_call(functools.partial(kernel, n_ctx, n_tp, rows), out_shape=(j...  59.4 us
    pallas_call x1, Pallas kernels, shards(): pl.pallas_call(finish, out_shape=(jax.ShapeDtypeStruct((rows, width), BF1...  2.38 us

profile of v2, /device:TPU:1, one launch (start us, length us, event | category | flops | bytes accessed | tf_op | source)
XLA Modules:
  0.0 62.6 jit_solution(3150677913595393219)
XLA Ops:
  0.6 59.4 %shard_map.153 = (bf16[512,1024]{1,0:T(8,128)(2,1)}, bf16[512,128]{1,0:T(8,128)(2,1)}, bf16[512,128]{1,0:T(8,128)(2,1)}, f32[2,8,640]{2,1,0:T(8,128)}, bf16[2,8,16,512]{3,2,1,0:T(8,128)(2,1)}) custom-call(bf16[512,8192]{1,0:T(8,128)(2,1)} %x_hbm.1, bf16[512,1024]{1,0:T(8,128)(2,1)} %q_hbm.1, bf16[512,128]{1,0:T(8,128)(2,1)} %k_hbm.1, ...), custom_call_target="tpu_custom_call" | custom-call | flops 12000000000 | bytes 16000000 | tf_op jit(solution)/shard_map/pallas_call | solution.py:700
  60.1 2.4 %shard_map.154 = (bf16[512,1024]{1,0:T(8,128)(2,1)}, bf16[512,128]{1,0:T(8,128)(2,1)}, bf16[512,128]{1,0:T(8,128)(2,1)}, f32[8,8192]{1,0:T(8,128)}, f32[8,1024]{...) custom-call(bf16[512,1024]{1,0:T(8,128)(2,1)} %get-tuple-element.12.dq_in, bf16[512,128]{1,0:T(8,128)(2,1)} %get-tuple-element.13.gk_in, ...), custom_call_target="tpu_custom_call" | custom-call | tf_op jit(solution)/shard_map/pallas_call | solution.py:776
